TPU v7x, 32 devices: a whole 2x2x4 slice. The times are simulated.
32 devices in a mesh: section: 2 (over y), dp: 4 (over x, core), tensor: 4 (over z).
Axes of the slice: x: 2, y: 2, z: 4, core: 2. Of those that a mesh axis runs over, the one named last changes fastest.
Arguments:
- inputs: bfloat16 [2, 1024, 12288], P('section', 'dp', 'tensor'), may hold values from -6 to 6
- queries: bfloat16 [2, 1024, 1024], P('section', 'dp', 'tensor'), may hold values from -8 to 8
- keys: bfloat16 [2, 1024, 1024], P('section', 'dp', 'tensor'), may hold values from -8 to 8
- w_value: bfloat16 [2, 12288, 1024], P('section', None, 'tensor'), may hold values from -0.0546875 to 0.0546875
- w_out: bfloat16 [2, 1024, 12288], P('section', 'tensor'), may hold values from -0.5 to 0.5
Outputs:
- next_inputs: bfloat16 [2, 1024, 12288], P('section', 'dp', 'tensor')
All inputs are finite; a program needn't handle non-finite values.
Results may differ from a plain program's by a relative error of at most 0.023.
Values may be sent and summed in bfloat16 or wider, within the bound.
A program may use at most 64 MiB of HBM per device.

v0:
```python
import jax
import jax.numpy as jnp
from jax import lax
from jax.sharding import PartitionSpec as P

HEAD_SIZE = 128
LEN = 256


def partner(value, axis, stride):
    mask = 2**stride
    pairs = [(source, source ^ mask) for source in range(lax.axis_size(axis))]
    return lax.ppermute(value, axis, pairs)


def on_device(inputs, queries, keys, w_value, w_out):
    activ = inputs[0]
    weight_v = w_value[0]
    weight_o = w_out[0]
    length = activ.shape[0]
    col_width = activ.shape[1]
    features_all = lax.all_gather(activ, "tensor", axis=1, tiled=True)
    values = jnp.dot(features_all, weight_v, preferred_element_type=jnp.float32)
    values = values.astype(jnp.bfloat16)
    heads_here = weight_v.shape[1] // HEAD_SIZE
    query_rows = queries[0].reshape(length // LEN, LEN, heads_here, HEAD_SIZE)
    key_rows = keys[0].reshape(length // LEN, LEN, heads_here, HEAD_SIZE)
    value_rows = values.reshape(length // LEN, LEN, heads_here, HEAD_SIZE)
    scores = jnp.einsum(
        "bqhd,bkhd->bhqk", query_rows, key_rows, preferred_element_type=jnp.float32
    ) / jnp.sqrt(jnp.float32(HEAD_SIZE))
    rows = lax.broadcasted_iota(jnp.int32, (LEN, LEN), 0)
    cols = lax.broadcasted_iota(jnp.int32, (LEN, LEN), 1)
    scores = jnp.where((cols <= rows)[None, None], scores, jnp.float32(-1e30))
    top = jnp.max(scores, axis=-1, keepdims=True)
    expo = jnp.exp(scores - top)
    probs = (expo / jnp.sum(expo, axis=-1, keepdims=True)).astype(jnp.bfloat16)
    context = jnp.einsum(
        "bhqk,bkhd->bqhd", probs, value_rows, preferred_element_type=jnp.float32
    ).astype(jnp.bfloat16)
    context = context.reshape(length, heads_here * HEAD_SIZE)
    partial_term = jnp.dot(context, weight_o, preferred_element_type=jnp.float32)
    total = lax.psum(partial_term.astype(jnp.bfloat16), "tensor").astype(jnp.float32)
    mine = lax.dynamic_slice_in_dim(total, lax.axis_index("tensor") * col_width, col_width, 1)
    result = (mine + activ.astype(jnp.float32)).astype(jnp.bfloat16)
    passed = partner(result, "section", 0)
    return passed[None]


def solution(mesh):
    return jax.shard_map(
        on_device,
        mesh=mesh,
        in_specs=(
            P("section", "dp", "tensor"),
            P("section", "dp", "tensor"),
            P("section", "dp", "tensor"),
            P("section", None, "tensor"),
            P("section", "tensor", None),
        ),
        out_specs=P("section", "dp", "tensor"),
        check_vma=False,
    )
```

profile of v0, /device:TPU:0, one launch (start us, length us, event | category | flops | bytes accessed | tf_op | source)
XLA Modules:
  0.0 409.1 jit_solution(16850483974988070047)
XLA Ops:
  6.5 0.0 all-gather.3.cloned.1.call-start
  6.5 0.7 all-gather.3.cloned.1.call-update
  7.3 0.0 all-reduce.2.cloned.1.call-start
  7.3 0.9 reshape.47
  8.2 0.9 reshape.48
  9.2 0.3 fusion.23
  9.6 0.2 fusion.8
  9.8 117.2 %all-gather.3.cloned.1.call-done = bf16[1,256,12288]{2,1,0:T(8,128)(2,1)} async-done(((bf16[1,256,3072]{2,1,0:T(8,128)(2,1)}), bf16[1,256,12288]{2,1,0:T(8,128)(2,1)}) %all-gather.3.cloned.1.call-update) | async-done | bytes 6291472 | tf_op jit(solution)/shard_map/all_gather | solution.py:22
  127.0 7.1 %fusion.9 = bf16[256,256]{0,1:T(8,128)(2,1)S(1)} fusion(bf16[1,12288,256]{2,1,0:T(8,128)(2,1)} %param.8, bf16[1,256,12288]{2,1,0:T(8,128)(2,1)} %all-gather.3.cloned.1.call-done), kind=kOutput, calls=%fused_computation.13 | convolution fusion | flops 1610678272 | bytes 12713984 | tf_op jit(solution)/shard_map/dot_general | solution.py:23
  134.2 0.3 convolution_convert_fusion.1
  134.5 7.3 %convolution_convert_fusion = bf16[256,12288]{1,0:T(8,128)(2,1)} fusion(bf16[256,256]{0,1:T(8,128)(2,1)S(1)} %bitcast.28, bf16[1,256,12288]{2,1,0:T(8,128)(2,1)} %param.9), kind=kOutput, calls=%fused_computation.1 | convolution fusion | flops 1613758464 | bytes 12713984 | tf_op jit(solution)/shard_map/dot_general | solution.py:42
  141.7 0.0 copy-start
  141.7 0.0 all-reduce.2.cloned.1.call-update
  141.8 221.2 %all-reduce.2.cloned.1.call-done = bf16[256,12288]{1,0:T(8,128)(2,1)} async-done(((bf16[256,12288]{1,0:T(8,128)(2,1)}), bf16[256,12288]{1,0:T(8,128)(2,1)}) %all-reduce.2.cloned.1.call-update) | async-done | bytes 6291472 | tf_op jit(solution)/shard_map/psum | solution.py:43
  363.0 0.0 copy-done
  363.0 2.0 fusion.5
  364.9 1.5 collective-permute-start
  366.5 34.7 %collective-permute-done = bf16[256,3072]{1,0:T(8,128)(2,1)S(1)} collective-permute-done((bf16[256,3072]{1,0:T(8,128)(2,1)S(1)}, bf16[256,3072]{1,0:T(8,128)(2,1)S(1)}, u32[]{:S(2)}, u32[]{:S(2)}) %collective-permute-start) | collective-permute-done | bytes 1572896 | tf_op jit(solution)/shard_map/ppermute | solution.py:13
  401.1 1.1 copy.24
  (1 shorter events, 0.0 us)
Async XLA Ops:
  6.5 120.5 %all-gather.3.cloned.1.call-start = ((), (), s32[]{:S(2)}) async-start(), calls=%async_computation.1 | async-start | bytes 7864320 | tf_op jit(solution)/shard_map/all_gather | solution.py:22
  7.3 355.7 %all-reduce.2.cloned.1.call-start = ((), (), s32[]{:S(2)}) async-start(), calls=%async_computation | async-start | bytes 12582912 | tf_op jit(solution)/shard_map/psum | solution.py:43
  141.7 221.2 %copy-start = (bf16[1,256,3072]{2,1,0:T(8,128)(2,1)S(1)}, bf16[1,256,3072]{2,1,0:T(8,128)(2,1)}, u32[]{:S(2)}) copy-start(bf16[1,256,3072]{2,1,0:T(8,128)(2,1)} %param.5) | copy-start | bytes 4718596
  364.9 36.2 %collective-permute-start = (bf16[256,3072]{1,0:T(8,128)(2,1)S(1)}, bf16[256,3072]{1,0:T(8,128)(2,1)S(1)}, u32[]{:S(2)}, u32[]{:S(2)}) collective-permute-start(bf16[256,3072]{1,0:T(8,128)(2,1)S(1)} %fusion.5), channel_id=1, source_target_pairs={{0,16},{16,0},{1,17},{17,1},{2,18},{18,2},{3,19},{19,3},{4,20},{20... | collective-permute-start | bytes 4718600 | tf_op jit(solution)/shard_map/ppermute | solution.py:13
Sparse Core Ops, SparseCore 0:
  8.9 118.0 all-gather.2
  141.9 221.0 all-reduce.1
where the time goes:
time: 409 us
  waiting for transfers between devices  374 us (91%)
  matrix products  15.3 us (4%)
  between operations  13.4 us (3%)
    psum x1, waiting for transfers between devices, on_device(): lax.psum(partial_term.astype(jnp.bfloat16), 'tensor').astype(jnp.float32)  221 us
    all_gather x1, waiting for transfers between devices, on_device(): features_all = lax.all_gather(activ, 'tensor', axis=1, tiled=True)  117 us
    ppermute x1, waiting for transfers between devices, partner(): return lax.ppermute(value, axis, pairs)  34.7 us
  transfers between devices with their start and end apart: 3, of which 3 were waited for; matrix products, arithmetic and copies ran while one was open for 1% of the time, Pallas kernels for 0%

commit v1 on v0

--- a/solution.py
+++ b/solution.py
@@ -1,19 +1,269 @@
+import functools
+
 import jax
 import jax.numpy as jnp
 from jax import lax
+from jax.experimental import pallas as pl
+from jax.experimental.pallas import tpu as pltpu
 from jax.sharding import PartitionSpec as P
 
 HEAD_SIZE = 128
 LEN = 256
-
-
-def partner(value, axis, stride):
-    mask = 2**stride
-    pairs = [(source, source ^ mask) for source in range(lax.axis_size(axis))]
-    return lax.ppermute(value, axis, pairs)
-
-
-def on_device(inputs, queries, keys, w_value, w_out):
+V_SUB = 2
+O_SUB = 2
+WINDOW = 3
+ORDER = (2, 1, 3)
+
+
+def flip(index, bit):
+    step = 2**bit
+    return index + step - 2 * step * lax.rem(index // step, 2)
+
+
+def flip_by(index, mask):
+    for bit in range(mask.bit_length()):
+        if mask >> bit & 1:
+            index = flip(index, bit)
+    return index
+
+
+def moving_weights(
+    n,
+    activ_hbm, query_hbm, key_hbm, wv_hbm, wo_hbm, out_hbm,
+    activ, query, key, wv, wo, part_out, part_in, context, result,
+    local_sem, wv_send, wv_recv, wo_send, wo_recv, small_send, small_recv, out_send, out_recv,
+):
+    section = lax.axis_index("section")
+    dp = lax.axis_index("dp")
+    z = lax.axis_index("tensor")
+    length, cols = activ.shape
+    quarter = cols // 4
+    v_rows = quarter // V_SUB
+    o_cols = quarter // O_SUB
+    core_peer = flip(dp, 0)
+    chip_peer = flip(dp, 1)
+    diagonal = flip(core_peer, 1)
+    quarters = (dp, core_peer, chip_peer, diagonal)
+    other = flip(section, 0)
+
+    barrier = pltpu.get_barrier_semaphore()
+    for slot in range(1, n):
+        pl.semaphore_signal(barrier, inc=1, device_id=(section, dp, flip_by(z, slot)),
+                            device_id_type=pl.DeviceIdType.MESH)
+    for target in ((section, core_peer, z), (section, chip_peer, z), (other, dp, z)):
+        pl.semaphore_signal(barrier, inc=1, device_id=target, device_id_type=pl.DeviceIdType.MESH)
+
+    def remote(src, dst, send, recv, target):
+        return pltpu.make_async_remote_copy(
+            src_ref=src, dst_ref=dst, send_sem=send, recv_sem=recv,
+            device_id=target, device_id_type=pl.DeviceIdType.MESH)
+
+    own = pl.multiple_of(z * cols, cols)
+    locals_ = [
+        pltpu.make_async_copy(activ_hbm.at[0], activ, local_sem.at[0]),
+        pltpu.make_async_copy(query_hbm.at[0], query, local_sem.at[1]),
+        pltpu.make_async_copy(key_hbm.at[0], key, local_sem.at[2]),
+        pltpu.make_async_copy(wv_hbm.at[0, pl.ds(own, cols), :], wv.at[0], local_sem.at[3]),
+        pltpu.make_async_copy(wo_hbm.at[0, :, pl.ds(own, cols)], wo.at[0], local_sem.at[4]),
+    ]
+    pl.semaphore_wait(barrier, n + 2)
+
+    pieces = [("v", slot, sub) for sub in range(V_SUB) for slot in ORDER]
+    n_value = len(pieces)
+    pieces += [("o", slot, sub) for sub in range(O_SUB) for slot in ORDER]
+
+    def v_at(slot, which, sub):
+        rows = pl.ds(pl.multiple_of(which * quarter + sub * v_rows, v_rows), v_rows)
+        return wv.at[slot, rows, :]
+
+    def o_at(slot, which, sub):
+        columns = pl.ds(pl.multiple_of(which * quarter + sub * o_cols, o_cols), o_cols)
+        return wo.at[slot, :, columns]
+
+    def copies(piece):
+        kind, slot, sub = piece
+        peer = flip_by(z, slot)
+        if kind == "v":
+            start = pl.multiple_of(peer * cols + dp * quarter + sub * v_rows, v_rows)
+            source = wv_hbm.at[0, pl.ds(start, v_rows), :]
+            at, send, recv = v_at, wv_send, wv_recv
+        else:
+            start = pl.multiple_of(peer * cols + dp * quarter + sub * o_cols, o_cols)
+            source = wo_hbm.at[0, :, pl.ds(start, o_cols)]
+            at, send, recv = o_at, wo_send, wo_recv
+        mine, far = at(slot, dp, sub), at(slot, chip_peer, sub)
+        def sems(hop):
+            return send.at[slot - 1, sub, hop], recv.at[slot - 1, sub, hop]
+        return (
+            remote(source, mine, *sems(0), (section, dp, peer)),
+            remote(mine, mine, *sems(1), (section, core_peer, z)),
+            remote(mine, mine, *sems(2), (section, chip_peer, z)),
+            remote(far, far, *sems(3), (section, core_peer, z)),
+        )
+
+    plan = [copies(piece) for piece in pieces]
+    for i in range(WINDOW):
+        plan[i][0].start()
+    for copy in locals_:
+        copy.start()
+
+    def step(i):
+        plan[i][0].wait_recv()
+        plan[i][2].start()
+        plan[i][1].start()
+        if i + WINDOW < len(plan):
+            plan[i][0].wait_send()
+            plan[i + WINDOW][0].start()
+        if i > 0:
+            relay(i - 1)
+
+    def relay(i):
+        plan[i][2].wait_recv()
+        plan[i][3].start()
+
+    def arrived(i):
+        plan[i][1].wait_recv()
+        plan[i][3].wait_recv()
+
+    for i in range(n_value):
+        step(i)
+    relay(n_value - 1)
+    for i in range(n_value):
+        arrived(i)
+    locals_[0].wait()
+    locals_[3].wait()
+
+    value_sends = []
+    for slot in ORDER + (0,):
+        term = jnp.dot(activ[...], wv[slot], preferred_element_type=jnp.float32)
+        if slot == 0:
+            mine_term = term
+        else:
+            part_out[slot - 1] = term.astype(jnp.bfloat16)
+            copy = remote(part_out.at[slot - 1], part_in.at[slot - 1], small_send.at[0, slot - 1],
+                          small_recv.at[0, slot - 1], (section, dp, flip_by(z, slot)))
+            copy.start()
+            value_sends.append(copy)
+    locals_[1].wait()
+    locals_[2].wait()
+
+    total = mine_term
+    for copy in value_sends:
+        copy.wait_recv()
+    for slot in range(1, n):
+        total = total + part_in[slot - 1].astype(jnp.float32)
+    values = total.astype(jnp.bfloat16)
+
+    causal = lax.broadcasted_iota(jnp.int32, (LEN, LEN), 1) <= lax.broadcasted_iota(jnp.int32, (LEN, LEN), 0)
+    scale = 1.0 / HEAD_SIZE**0.5
+    for start in range(0, length, LEN):
+        for head in range(0, query.shape[1], HEAD_SIZE):
+            rows, span = slice(start, start + LEN), slice(head, head + HEAD_SIZE)
+            scores = lax.dot_general(query[rows, span], key[rows, span], (((1,), (1,)), ((), ())),
+                                     preferred_element_type=jnp.float32) * scale
+            scores = jnp.where(causal, scores, -1e30)
+            expo = jnp.exp(scores - jnp.max(scores, axis=-1, keepdims=True))
+            probs = (expo / jnp.sum(expo, axis=-1, keepdims=True)).astype(jnp.bfloat16)
+            context[0, rows, span] = jnp.dot(
+                probs, values[rows, span], preferred_element_type=jnp.float32).astype(jnp.bfloat16)
+
+    context_sends = []
+    for slot in ORDER:
+        copy = remote(context.at[0], context.at[slot], small_send.at[1, slot - 1],
+                      small_recv.at[1, slot - 1], (section, dp, flip_by(z, slot)))
+        copy.start()
+        context_sends.append(copy)
+
+    locals_[4].wait()
+    out_sends = []
+    per_sub = n - 1
+    done = n_value
+    for sub in range(O_SUB):
+        for i in range(done, done + per_sub):
+            plan_first = i == n_value
+            plan[i][0].wait_recv()
+            plan[i][2].start()
+            plan[i][1].start()
+            if i + WINDOW < len(plan):
+                plan[i][0].wait_send()
+                plan[i + WINDOW][0].start()
+            if not plan_first:
+                if i > done:
+                    relay(i - 1)
+        relay(done + per_sub - 1)
+        if sub == 0:
+            for copy in context_sends:
+                copy.wait_recv()
+        for order, which in enumerate(quarters):
+            for i in range(done, done + per_sub):
+                if order == 1:
+                    plan[i][1].wait_recv()
+                elif order == 3:
+                    plan[i][3].wait_recv()
+            start = pl.multiple_of(which * quarter + sub * o_cols, o_cols)
+            columns = pl.ds(start, o_cols)
+            total = activ[:, columns].astype(jnp.float32)
+            for slot in range(n):
+                total = total + jnp.dot(context[slot], wo[slot, :, columns],
+                                        preferred_element_type=jnp.float32)
+            result[sub * 4 + order] = total.astype(jnp.bfloat16)
+            copy = remote(result.at[sub * 4 + order], out_hbm.at[0, :, columns],
+                          out_send.at[sub * 4 + order], out_recv.at[sub * 4 + order], (other, dp, z))
+            copy.start()
+            out_sends.append(copy)
+        done += per_sub
+
+    for i, piece in enumerate(plan):
+        if i + WINDOW >= len(plan):
+            piece[0].wait_send()
+        for copy in piece[1:]:
+            copy.wait_send()
+    for copy in value_sends + context_sends:
+        copy.wait_send()
+    for copy in out_sends:
+        copy.wait()
+
+
+def by_weights(n, inputs, queries, keys, w_value, w_out):
+    length, cols = inputs.shape[1:]
+    width = w_value.shape[2]
+    bf16, dma = jnp.bfloat16, pltpu.SemaphoreType.DMA
+    chunks = 4 * O_SUB
+    return pl.pallas_call(
+        functools.partial(moving_weights, n),
+        out_shape=jax.ShapeDtypeStruct(inputs.shape, bf16),
+        in_specs=[pl.BlockSpec(memory_space=pl.ANY)] * 5,
+        out_specs=pl.BlockSpec(memory_space=pl.ANY),
+        scratch_shapes=[
+            pltpu.VMEM((length, cols), bf16),
+            pltpu.VMEM((length, width), bf16),
+            pltpu.VMEM((length, width), bf16),
+            pltpu.VMEM((n, cols, width), bf16),
+            pltpu.VMEM((n, width, cols), bf16),
+            pltpu.VMEM((n - 1, length, width), bf16),
+            pltpu.VMEM((n - 1, length, width), bf16),
+            pltpu.VMEM((n, length, width), bf16),
+            pltpu.VMEM((chunks, length, cols // chunks), bf16),
+            dma((5,)),
+            dma((n - 1, V_SUB, 4)),
+            dma((n - 1, V_SUB, 4)),
+            dma((n - 1, O_SUB, 4)),
+            dma((n - 1, O_SUB, 4)),
+            dma((2, n - 1)),
+            dma((2, n - 1)),
+            dma((chunks,)),
+            dma((chunks,)),
+        ],
+        compiler_params=pltpu.CompilerParams(
+            collective_id=0, has_side_effects=True, vmem_limit_bytes=48 * 2**20),
+        cost_estimate=pl.CostEstimate(
+            flops=4 * length * cols * n * width, bytes_accessed=2 * 4 * n * cols * width,
+            transcendentals=length * LEN * width // HEAD_SIZE),
+        name="weights_to_activations",
+    )(inputs, queries, keys, w_value, w_out)
+
+
+def by_activations(inputs, queries, keys, w_value, w_out):
     activ = inputs[0]
     weight_v = w_value[0]
     weight_o = w_out[0]
@@ -40,14 +290,26 @@
     ).astype(jnp.bfloat16)
     context = context.reshape(length, heads_here * HEAD_SIZE)
     partial_term = jnp.dot(context, weight_o, preferred_element_type=jnp.float32)
-    total = lax.psum(partial_term.astype(jnp.bfloat16), "tensor").astype(jnp.float32)
-    mine = lax.dynamic_slice_in_dim(total, lax.axis_index("tensor") * col_width, col_width, 1)
-    result = (mine + activ.astype(jnp.float32)).astype(jnp.bfloat16)
-    passed = partner(result, "section", 0)
-    return passed[None]
+    total = lax.psum_scatter(
+        partial_term.astype(jnp.bfloat16), "tensor", scatter_dimension=1, tiled=True)
+    result = (total.astype(jnp.float32) + activ.astype(jnp.float32)).astype(jnp.bfloat16)
+    size = lax.axis_size("section")
+    return lax.ppermute(result, "section", [(i, i ^ 1) for i in range(size)])[None]
 
 
 def solution(mesh):
+    n = mesh.shape["tensor"]
+
+    def on_device(inputs, queries, keys, w_value, w_out):
+        length, cols = inputs.shape[1:]
+        width = w_value.shape[2]
+        weights_smaller = n * width <= mesh.shape["dp"] * length
+        divides = (cols % (4 * 128 * O_SUB) == 0 and cols % (4 * 16 * V_SUB) == 0
+                   and length % LEN == 0 and n == len(ORDER) + 1 and mesh.shape["dp"] == 4)
+        if weights_smaller and divides:
+            return by_weights(n, inputs, queries, keys, w_value, w_out)
+        return by_activations(inputs, queries, keys, w_value, w_out)
+
     return jax.shard_map(
         on_device,
         mesh=mesh,

time: 409 us -> 130 us (0.32)
  waiting for transfers between devices: 374 us -> 0 us
  Pallas kernels: 0 us -> 125 us
  matrix products: 15.3 us -> 0 us
  between operations: 13.4 us -> 0.01 us
    psum x1 -> x0, waiting for transfers between devices: 221 us -> none  [on_device(): lax.psum(partial_term.astype(jnp.bfloat16), 'tensor').astype(jnp.float32)]
    pallas_call x0 -> x1, Pallas kernels: none -> 125 us  [by_weights(): pl.pallas_call(functools.partial(moving_weights, n), out_shape=jax.ShapeD...]
    all_gather x1 -> x0, waiting for transfers between devices: 117 us -> none  [on_device(): features_all = lax.all_gather(activ, 'tensor', axis=1, tiled=True)]
    ppermute x1 -> x0, waiting for transfers between devices: 34.7 us -> none  [partner(): return lax.ppermute(value, axis, pairs)]
    dot_general x4 -> x0, matrix products: 14.9 us -> none  [the longest x1 7.27 us: on_device(): jnp.dot(context, weight_o, preferred_element_type=jnp.float32)]
  transfers between devices with their start and end apart: 3 -> 0, of which waited for: 3 -> 0; matrix products, arithmetic and copies ran while one was open for 1% -> 0% of each run, Pallas kernels for 0% -> 0%
where the time goes in v1:
time: 130 us
  Pallas kernels  125 us (96%)
  local copies, waits for them, and re-layouts  4.36 us (3%)
    pallas_call x1, Pallas kernels, by_weights(): pl.pallas_call(functools.partial(moving_weights, n), out_shape=jax.ShapeD...  125 us
    unnamed x7, local copies, waits for them, and re-layouts  4.36 us

profile of v1, /device:TPU:0, one launch (start us, length us, event | category | flops | bytes accessed | tf_op | source)
XLA Modules:
  0.0 129.7 jit_solution(9405646333957672853)
XLA Ops:
  0.0 0.0 copy-start
  0.0 1.4 %copy-done = bf16[1,256,3072]{2,1,0:T(8,128)(2,1)S(1)} copy-done((bf16[1,256,3072]{2,1,0:T(8,128)(2,1)S(1)}, bf16[1,256,3072]{2,1,0:T(8,128)(2,1)}, u32[]{:S(2)}) %copy-start) | copy-done | bytes 1572888
  1.4 0.0 copy-start.1
  1.4 0.9 copy-done.1
  2.3 0.0 copy-start.2
  2.3 0.9 copy-done.2
  3.2 125.3 %weights_to_activations.1 = bf16[1,256,3072]{2,1,0:T(8,128)(2,1)S(1)} custom-call(bf16[1,256,3072]{2,1,0:T(8,128)(2,1)S(1)} %copy-done, bf16[1,256,256]{2,1,0:T(8,128)(2,1)S(1)} %copy-done.1, bf16[1,256,256]{2,1,0:T(8,128)(2,1)S(1)} %copy-done.2, bf16[1,12288,256]{2,1,0:T(8,128)(2,1)} %wv_hbm.1, bf16[1,256,12288]{2,1,0:T(8,128)(2,1)} %wo_hbm.1), custom_call_target="tpu_custom_call" | custom-call | flops 3221225472 | bytes 25165824 | tf_op jit(solution)/shard_map/weights_to_activations/pallas_call | solution.py:232
  128.5 1.1 copy.7
Async XLA Ops:
  0.0 1.4 %copy-start = (bf16[1,256,3072]{2,1,0:T(8,128)(2,1)S(1)}, bf16[1,256,3072]{2,1,0:T(8,128)(2,1)}, u32[]{:S(2)}) copy-start(bf16[1,256,3072]{2,1,0:T(8,128)(2,1)} %activ_hbm.1) | copy-start | bytes 4718596
  1.4 0.9 copy-start.1
  2.3 0.9 copy-start.2
